TPU v7x, 32 devices: a whole 2x2x4 slice. The times are simulated.
32 devices in a mesh: band: 4 (over y, x), tm: 8 (over z, core).
Axes of the slice: x: 2, y: 2, z: 4, core: 2. Of those that a mesh axis runs over, the one named last changes fastest.
Arguments:
- chebyshev: float32 [32, 3, 32768], P(None, None, ('band', 'tm')), may hold values from -0.9 to 0.9
- crossing: int32 [4, 2, 512], P('band'), may hold values from 0 to 4095, as said below
- counts: int32 [4], P('band'), may hold values from 4096 to 8192, as said below
- route: int32 [4, 32], P('band'), may hold values from 0 to 31, each once within a row
- pairs: int32 [4, 2, 32], P('band'), may hold values from 0 to 31, each once within a row
Outputs:
- closest: float32 [128, 256, 256], P('band', 'tm')
Inputs may be any that keep to these rules, and one draw needn't show every extreme that they name: `crossing`: the 1024 slots of one band are distinct and below 4096, so every band's live slots include them. `counts`: some band is full in every draw. `route`: each row is a permutation of the band's 32 tiles. `pairs`: each row of one owner is a permutation of its 32 received tiles.
All inputs are finite; a program needn't handle non-finite values.
Results may differ from a plain program's by a relative error of at most 0.0003.
Values sent between devices are 32-bit elements; how exact they have to be, the bound alone decides.
A program may use at most 64 MiB of HBM per device.

v0:
```python
import functools

import jax
import jax.numpy as jnp
import numpy as np
from jax import lax
from jax.experimental import pallas as pl
from jax.experimental.pallas import tpu as pltpu
from jax.sharding import PartitionSpec as P

SAMPLES = 64
HIGHEST = lax.Precision.HIGHEST


def shifted(block, axis, distance):
    devices = range(lax.axis_size(axis))
    route = [(i - distance, i) for i in devices if i - distance in devices]
    return lax.ppermute(block, axis, route)


def basis_table(order_count):
    times = -1.0 + (2.0 * np.arange(SAMPLES) + 1.0) / SAMPLES
    return np.cos(np.arange(order_count)[None, :] * np.arccos(times)[:, None])


def split3(values):
    high = values.astype(jnp.bfloat16)
    rest = values - high.astype(jnp.float32)
    middle = rest.astype(jnp.bfloat16)
    low = (rest - middle.astype(jnp.float32)).astype(jnp.bfloat16)
    return high, middle, low


def join3(product, rows):
    return (product[:rows] + product[rows : 2 * rows]) + product[2 * rows :]


def pick_kernel(slots_ref, shards_ref, rise_ref, fall_ref):
    steps, rows, width = shards_ref.shape
    ranks = slots_ref.shape[0]
    slot_ids = lax.broadcasted_iota(jnp.int32, (ranks, width), 1)
    total = None
    for step in range(steps):
        hit = slots_ref[...] - step * width == slot_ids
        one_hot = hit.astype(jnp.float32).astype(jnp.bfloat16)
        parts = jnp.concatenate(split3(shards_ref[step]), axis=0)
        product = lax.dot_general(
            parts, one_hot, (((1,), (1,)), ((), ())), preferred_element_type=jnp.float32
        )
        total = product if total is None else total + product
    joined = join3(total, rows)
    rise_ref[...] = joined[:, : ranks // 2]
    fall_ref[...] = joined[:, ranks // 2 :]


def pick(whole, slots_column, steps):
    _, rows, width = whole.shape
    ranks = slots_column.shape[0]
    half = jax.ShapeDtypeStruct((rows, ranks // 2), jnp.float32)
    return pl.pallas_call(
        pick_kernel,
        grid=(1,),
        in_specs=[
            pl.BlockSpec((ranks, 1), lambda i: (0, 0)),
            pl.BlockSpec((steps, rows, width), lambda i: (0, 0, 0)),
        ],
        out_specs=[pl.BlockSpec((rows, ranks // 2), lambda i: (0, 0))] * 2,
        out_shape=[half, half],
        compiler_params=pltpu.CompilerParams(vmem_limit_bytes=40 * 2**20),
        name="pick",
    )(slots_column, whole)


def place_kernel(crossing_tiles, route_ref, slots_ref, tile_ref, rise_ref, fall_ref, out_ref, parts):
    step = pl.program_id(0)
    rows, width = tile_ref.shape[1:]
    ranks = slots_ref.shape[0]
    tile_id = route_ref[step]

    @pl.when(step == 0)
    def _():
        joined = jnp.concatenate([rise_ref[...], fall_ref[...]], axis=1)
        parts[...] = jnp.concatenate(split3(joined), axis=0)

    @pl.when(tile_id >= crossing_tiles)
    def _():
        out_ref[...] = tile_ref[...]

    @pl.when(tile_id < crossing_tiles)
    def _():
        slot_ids = lax.broadcasted_iota(jnp.int32, (ranks, width), 1) + tile_id * width
        hit = (slots_ref[...] == slot_ids).astype(jnp.float32)
        one_hot = hit.astype(jnp.bfloat16)
        taken = jnp.sum(hit, axis=0, keepdims=True)
        product = jnp.dot(parts[...], one_hot, preferred_element_type=jnp.float32)
        out_ref[0] = jnp.where(taken > 0.0, join3(product, rows), tile_ref[0])


def place(whole, slots_column, climbers, sinkers, route, tile_size):
    _, rows, width = whole.shape
    ranks = slots_column.shape[0]
    tile_count = route.shape[0]
    per_shard = width // tile_size
    return pl.pallas_call(
        functools.partial(place_kernel, tile_count // 2),
        grid_spec=pltpu.PrefetchScalarGridSpec(
            num_scalar_prefetch=1,
            grid=(tile_count,),
            in_specs=[
                pl.BlockSpec((ranks, 1), lambda i, r: (0, 0)),
                pl.BlockSpec(
                    (1, rows, tile_size),
                    lambda i, r: (r[i] // per_shard, 0, r[i] % per_shard),
                ),
                pl.BlockSpec((rows, ranks // 2), lambda i, r: (0, 0)),
                pl.BlockSpec((rows, ranks // 2), lambda i, r: (0, 0)),
            ],
            out_specs=pl.BlockSpec((1, rows, tile_size), lambda i, r: (i, 0, 0)),
            scratch_shapes=[pltpu.VMEM((3 * rows, ranks), jnp.bfloat16)],
        ),
        out_shape=jax.ShapeDtypeStruct((tile_count, rows, tile_size), jnp.float32),
        compiler_params=pltpu.CompilerParams(vmem_limit_bytes=40 * 2**20),
        name="place",
    )(route, slots_column, whole, climbers, sinkers)


def pair_kernel(
    share,
    first_ids,
    second_ids,
    live,
    place_ref,
    window_ref,
    tile_ref,
    alive_window_ref,
    alive_tile_ref,
    table_ref,
    table_t_ref,
    out_ref,
    turned,
    first_pos,
    second_pos,
):
    step = pl.program_id(0)
    both = live[first_ids[step]] * live[second_ids[step]]

    @pl.when(both == 0)
    def _():
        out_ref[...] = jnp.zeros_like(out_ref)

    @pl.when(both != 0)
    def _():
        window = window_ref[0]
        rows, lanes = window.shape
        flags = jnp.broadcast_to(alive_window_ref[0], (8, lanes))
        turned[...] = jnp.concatenate([window, flags], axis=0).T
        mine = turned[pl.ds(pl.multiple_of(place_ref[1], share), share), :]
        first_pos[...] = jnp.dot(
            mine[:, :rows], table_t_ref[...], precision=HIGHEST, preferred_element_type=jnp.float32
        )
        second_pos[...] = jnp.dot(
            table_ref[...], tile_ref[0], precision=HIGHEST, preferred_element_type=jnp.float32
        )
        closest = None
        for s in range(SAMPLES):
            gaps = [
                first_pos[:, c * SAMPLES + s : c * SAMPLES + s + 1]
                - second_pos[c * SAMPLES + s : c * SAMPLES + s + 1, :]
                for c in range(3)
            ]
            square = (gaps[0] * gaps[0] + gaps[1] * gaps[1]) + gaps[2] * gaps[2]
            closest = square if closest is None else jnp.minimum(closest, square)
        out_ref[0] = closest * (mine[:, rows : rows + 1] * alive_tile_ref[0])


def pair_blocks(tiles, alive, first_ids, second_ids, row_start, share):
    tile_count, rows, tile_size = tiles.shape
    orders = rows // 3
    table = np.kron(np.eye(3), basis_table(orders)).astype(np.float32)
    live = (jnp.max(alive, axis=1) > 0.0).astype(jnp.int32)
    lanes = min(128, tile_size)
    position = jnp.stack([row_start // lanes, row_start % lanes]).astype(jnp.int32)
    alive = alive.reshape(tile_count, 1, tile_size)
    return pl.pallas_call(
        functools.partial(pair_kernel, share),
        grid_spec=pltpu.PrefetchScalarGridSpec(
            num_scalar_prefetch=4,
            grid=(tile_count,),
            in_specs=[
                pl.BlockSpec((1, rows, lanes), lambda i, a, b, l, w: (a[i], 0, w[0])),
                pl.BlockSpec((1, rows, tile_size), lambda i, a, b, l, w: (b[i], 0, 0)),
                pl.BlockSpec((1, 1, lanes), lambda i, a, b, l, w: (a[i], 0, w[0])),
                pl.BlockSpec((1, 1, tile_size), lambda i, a, b, l, w: (b[i], 0, 0)),
                pl.BlockSpec((3 * SAMPLES, rows), lambda i, a, b, l, w: (0, 0)),
                pl.BlockSpec((rows, 3 * SAMPLES), lambda i, a, b, l, w: (0, 0)),
            ],
            out_specs=pl.BlockSpec((1, share, tile_size), lambda i, a, b, l, w: (i, 0, 0)),
            scratch_shapes=[
                pltpu.VMEM((lanes, rows + 8), jnp.float32),
                pltpu.VMEM((share, 3 * SAMPLES), jnp.float32),
                pltpu.VMEM((3 * SAMPLES, tile_size), jnp.float32),
            ],
        ),
        out_shape=jax.ShapeDtypeStruct((tile_count, share, tile_size), jnp.float32),
        compiler_params=pltpu.CompilerParams(vmem_limit_bytes=40 * 2**20),
        name="pair_blocks",
    )(first_ids, second_ids, live, position, tiles, tiles, alive, alive, table, table.T)


def on_device(chebyshev, crossing, counts, route, pairs):
    orders, _, local = chebyshev.shape
    tm_count = lax.axis_size("tm")
    tile_count = route.shape[1]
    obj_count = local * tm_count
    tile_size = obj_count // tile_count
    share = tile_size // tm_count
    row_start = lax.axis_index("tm") * share

    flat = chebyshev.transpose(1, 0, 2).reshape(3 * orders, local)
    whole = lax.all_gather(flat, "tm", axis=0, tiled=False)

    slot_ids = jnp.arange(tile_size, dtype=jnp.int32)[None, :] + tile_size * route[0][:, None]
    alive_out = (slot_ids < counts[0]).astype(jnp.float32)
    alive = lax.all_to_all(alive_out, "band", split_axis=0, concat_axis=0, tiled=True)

    slots_column = crossing[0].reshape(-1, 1)
    rising, falling = pick(whole, slots_column, (tm_count + 1) // 2)
    climbers = shifted(rising, "band", 1)
    sinkers = shifted(falling, "band", -1)
    outgoing = place(whole, slots_column, climbers, sinkers, route[0], tile_size)
    tiles = lax.all_to_all(outgoing, "band", split_axis=0, concat_axis=0, tiled=True)
    return pair_blocks(tiles, alive, pairs[0, 0], pairs[0, 1], row_start, share)


def solution(mesh):
    placed = (
        P(None, None, ("band", "tm")),
        P("band", None, None),
        P("band"),
        P("band", None),
        P("band", None, None),
    )
    return jax.shard_map(
        on_device, mesh=mesh, in_specs=placed, out_specs=P("band", "tm", None), check_vma=False
    )
```

profile of v0, /device:TPU:4, one launch (start us, length us, event | category | flops | bytes accessed | tf_op | source)
XLA Modules:
  0.0 174.6 jit_solution(3211553457417424868)
XLA Ops:
  6.5 0.0 copy-start.7
  6.5 0.0 all-gather.2.cloned.1.call-start
  6.5 0.7 all-gather.2.cloned.1.call-update
  7.3 0.7 copy.12
  8.0 1.0 copy.13
  9.0 0.7 multiply_reduce_fusion
  9.7 0.1 mul.19
  10.4 38.1 %all-gather.2.cloned.1.call-done.shards_ref.tile_ref = f32[8,96,1024]{2,1,0:T(8,128)} async-done(((f32[1,96,1024]{2,1,0:T(8,128)}), f32[8,96,1024]{2,1,0:T(8,128)}) %all-gather.2.cloned.1.call-update) | async-done | bytes 3145744 | tf_op jit(solution)/shard_map/all_gather | solution.py:220
  48.5 0.0 copy-start.1
  48.5 1.9 %copy-done.1 = f32[8,96,1024]{2,1,0:T(8,128)S(1)} copy-done((f32[8,96,1024]{2,1,0:T(8,128)S(1)}, f32[8,96,1024]{2,1,0:T(8,128)}, u32[]{:S(2)}) %copy-start.1) | copy-done | bytes 3145752
  50.4 0.0 copy-start.3
  50.4 1.0 copy-done.3
  51.5 0.0 copy-start.2
  51.5 3.4 %pick.1 = (f32[96,512]{1,0:T(8,128)}, f32[96,512]{1,0:T(8,128)}) custom-call(s32[1024,1]{1,0:T(8,128)S(1)} %bitcast.15, f32[8,96,1024]{2,1,0:T(8,128)S(1)} %copy-done.1), custom_call_target="tpu_custom_call" | custom-call | tf_op jit(solution)/shard_map/pick/pallas_call | solution.py:60
  54.8 3.4 %collective-permute-start = (f32[96,512]{1,0:T(8,128)}, f32[96,512]{1,0:T(8,128)S(1)}, u32[]{:S(2)}, u32[]{:S(2)}) collective-permute-start(f32[96,512]{1,0:T(8,128)} %get-tuple-element.7), channel_id=1, source_target_pairs={{0,8},{8,16},{16,24},{1,9},{9,17},{17,25},{2,10},{10,18},{18,26},{... | collective-permute-start | bytes 589832 | tf_op jit(solution)/shard_map/ppermute | solution.py:18
  58.2 3.4 %collective-permute-start.1 = (f32[96,512]{1,0:T(8,128)}, f32[96,512]{1,0:T(8,128)S(1)}, u32[]{:S(2)}, u32[]{:S(2)}) collective-permute-start(f32[96,512]{1,0:T(8,128)} %get-tuple-element.8), channel_id=1, source_target_pairs={{8,0},{16,8},{24,16},{9,1},{17,9},{25,17},{10,2},{18,10},{26,18},{... | collective-permute-start | bytes 589832 | tf_op jit(solution)/shard_map/ppermute | solution.py:18
  61.6 0.7 fusion
  62.3 3.9 %all-to-all-start = ((f32[4,8,256]{2,1,0:T(8,128)}), f32[4,8,256]{2,1,0:T(8,128)}, u32[]{:S(2)}, u32[]{:S(2)}) async-start(f32[4,8,256]{2,1,0:T(8,128)} %fusion), calls=%async_computation | async-start | bytes 65536 | tf_op jit(solution)/shard_map/all_to_all | solution.py:224
  66.1 0.0 collective-permute-done.rise_ref
  66.1 1.3 collective-permute-done.1.fall_ref
  67.4 0.0 copy-done.7
  67.5 0.0 copy-done.2
  67.5 0.0 copy-start.4
  67.5 1.0 copy-done.4
  68.5 9.4 %place.1 = f32[32,96,256]{2,1,0:T(8,128)S(1)} custom-call(s32[32]{0:T(128)S(1)} %bitcast.17, s32[1024,1]{1,0:T(8,128)S(1)} %bitcast.16, f32[8,96,1024]{2,1,0:T(8,128)S(1)} %copy-done.2, f32[96,512]{1,0:T(8,128)S(1)} %collective-permute-done.rise_ref, f32[96,512]{1,0:T(8,128)S(1)} %collective-permute-done.1.fall_ref), custom_call_target="tpu_custom_call" | custom-call | tf_op jit(solution)/shard_map/place/pallas_call | solution.py:104
  77.9 0.0 copy-start
  78.0 1.6 copy-done
  79.6 0.0 copy-start.8
  79.6 0.0 copy-start.5
  79.6 0.0 copy-start.6
  79.6 0.0 all-to-all-done
  79.6 6.2 %all-to-all-start.1 = ((f32[32,96,256]{2,1,0:T(8,128)}), f32[32,96,256]{2,1,0:T(8,128)S(1)}, u32[]{:S(2)}, u32[]{:S(2)}) async-start(f32[32,96,256]{2,1,0:T(8,128)} %copy-done), calls=%async_computation.1 | async-start | bytes 6291456 | tf_op jit(solution)/shard_map/all_to_all | solution.py:231
  85.8 0.1 pad_add_fusion.place_ref
  85.9 0.0 copy-done.8
  85.9 0.8 reduce_max.9
  86.7 0.1 reshape.29.live
  86.8 0.8 reshape.28.alive_window_ref.alive_tile_ref
  87.6 33.4 %all-to-all-done.1.window_ref.tile_ref = f32[32,96,256]{2,1,0:T(8,128)S(1)} async-done(((f32[32,96,256]{2,1,0:T(8,128)}), f32[32,96,256]{2,1,0:T(8,128)S(1)}, u32[]{:S(2)}, u32[]{:S(2)}) %all-to-all-start.1) | async-done | bytes 3145760 | tf_op jit(solution)/shard_map/all_to_all | solution.py:231
  121.0 0.0 copy-done.5
  121.0 0.0 copy-done.6
  121.0 46.8 %pair_blocks.1 = f32[32,32,256]{2,1,0:T(8,128)} custom-call(s32[32]{0:T(128)S(1)} %get-tuple-element.10.first_ids, s32[32]{0:T(128)S(1)} %get-tuple-element.9.second_ids, s32[32]{0:T(128)S(1)} %reshape.29.live, s32[2]{0:T(128)S(1)} %pad_add_fusion.place_ref, f32[32,96,256]{2,1,0:T(8,128)S(1)} %all-to-all-done.1.window_ref.tile_ref, ...), custom_call_target="tpu_custom_call" | custom-call | tf_op jit(solution)/shard_map/pair_blocks/pallas_call | solution.py:184
  (2 shorter events, 0.0 us)
Async XLA Ops:
  6.5 60.9 %copy-start.7 = (s32[1,32]{1,0:T(1,128)S(1)}, s32[1,32]{1,0:T(1,128)}, u32[]{:S(2)}) copy-start(s32[1,32]{1,0:T(1,128)} %param.10) | copy-start | bytes 388
  6.5 42.0 %all-gather.2.cloned.1.call-start = ((), (), s32[]{:S(2)}) async-start(), calls=%async_computation.2 | async-start | bytes 3538944 | tf_op jit(solution)/shard_map/all_gather | solution.py:220
  48.5 1.9 %copy-start.1 = (f32[8,96,1024]{2,1,0:T(8,128)S(1)}, f32[8,96,1024]{2,1,0:T(8,128)}, u32[]{:S(2)}) copy-start(f32[8,96,1024]{2,1,0:T(8,128)} %all-gather.2.cloned.1.call-done.shards_ref.tile_ref) | copy-start | bytes 9437188
  50.4 1.0 copy-start.3
  51.5 16.0 %copy-start.2 = (f32[8,96,1024]{2,1,0:T(8,128)S(1)}, f32[8,96,1024]{2,1,0:T(8,128)}, u32[]{:S(2)}) copy-start(f32[8,96,1024]{2,1,0:T(8,128)} %all-gather.2.cloned.1.call-done.shards_ref.tile_ref) | copy-start | bytes 9437188
  54.8 11.3 %collective-permute-start = (f32[96,512]{1,0:T(8,128)}, f32[96,512]{1,0:T(8,128)S(1)}, u32[]{:S(2)}, u32[]{:S(2)}) collective-permute-start(f32[96,512]{1,0:T(8,128)} %get-tuple-element.7), channel_id=1, source_target_pairs={{0,8},{8,16},{16,24},{1,9},{9,17},{17,25},{2,10},{10,18},{18,26},{... | collective-permute-start | bytes 589832 | tf_op jit(solution)/shard_map/ppermute | solution.py:18
  58.2 9.2 %collective-permute-start.1 = (f32[96,512]{1,0:T(8,128)}, f32[96,512]{1,0:T(8,128)S(1)}, u32[]{:S(2)}, u32[]{:S(2)}) collective-permute-start(f32[96,512]{1,0:T(8,128)} %get-tuple-element.8), channel_id=1, source_target_pairs={{8,0},{16,8},{24,16},{9,1},{17,9},{25,17},{10,2},{18,10},{26,18},{... | collective-permute-start | bytes 589832 | tf_op jit(solution)/shard_map/ppermute | solution.py:18
  62.3 17.3 %all-to-all-start = ((f32[4,8,256]{2,1,0:T(8,128)}), f32[4,8,256]{2,1,0:T(8,128)}, u32[]{:S(2)}, u32[]{:S(2)}) async-start(f32[4,8,256]{2,1,0:T(8,128)} %fusion), calls=%async_computation | async-start | bytes 65536 | tf_op jit(solution)/shard_map/all_to_all | solution.py:224
  67.5 1.0 copy-start.4
  77.9 1.6 copy-start
  79.6 6.3 %copy-start.8 = (s32[1,2,32]{2,1,0:T(2,128)S(1)}, s32[1,2,32]{2,1,0:T(2,128)}, u32[]{:S(2)}) copy-start(s32[1,2,32]{2,1,0:T(2,128)} %param.11) | copy-start | bytes 772
  79.6 41.4 %copy-start.5 = (f32[192,96]{1,0:T(8,128)S(1)}, f32[192,96]{1,0:T(8,128)}, u32[]{:S(2)}) copy-start(f32[192,96]{1,0:T(8,128)} %constant.42.clone.table_ref) | copy-start | bytes 221188
  79.6 41.4 %copy-start.6 = (f32[96,192]{1,0:T(8,128)S(1)}, f32[96,192]{1,0:T(8,128)}, u32[]{:S(2)}) copy-start(f32[96,192]{1,0:T(8,128)} %constant.43.clone.table_t_ref) | copy-start | bytes 221188
  79.6 41.4 %all-to-all-start.1 = ((f32[32,96,256]{2,1,0:T(8,128)}), f32[32,96,256]{2,1,0:T(8,128)S(1)}, u32[]{:S(2)}, u32[]{:S(2)}) async-start(f32[32,96,256]{2,1,0:T(8,128)} %copy-done), calls=%async_computation.1 | async-start | bytes 6291456 | tf_op jit(solution)/shard_map/all_to_all | solution.py:231
Sparse Core Ops, SparseCore 0:
  9.0 39.4 all-gather.1
where the time goes:
time: 173 us; the launch traced here: 175 us
  waiting for transfers between devices  73.6 us (43%)
  Pallas kernels  59.6 us (34%)
  starting transfers between devices  16.8 us (10%)
  between operations  14.1 us (8%)
  local copies, waits for them, and re-layouts  8.3 us (5%)
  other arithmetic  2.29 us (1%)
    pallas_call x1, Pallas kernels, pair_blocks(): pl.pallas_call(functools.partial(pair_kernel, share), grid_spec=pltpu.Pre...  46.8 us
    all_gather x1, waiting for transfers between devices, on_device(): whole = lax.all_gather(flat, 'tm', axis=0, tiled=False)  38.1 us
    all_to_all x1, waiting for transfers between devices, on_device(): lax.all_to_all(outgoing, 'band', split_axis=0, concat_axis=0, tiled=True)  33.4 us
    pallas_call x1, Pallas kernels, place(): pl.pallas_call(functools.partial(place_kernel, tile_count // 2), grid_spe...  9.44 us
    unnamed x20, local copies, waits for them, and re-layouts  7.34 us
    ppermute x2, starting transfers between devices, shifted(): return lax.ppermute(block, axis, route)  6.73 us
    all_to_all x1, starting transfers between devices, on_device(): lax.all_to_all(outgoing, 'band', split_axis=0, concat_axis=0, tiled=True)  6.19 us
    all_to_all x1, starting transfers between devices, on_device(): lax.all_to_all(alive_out, 'band', split_axis=0, concat_axis=0, tiled=True)  3.86 us
  transfers between devices with their start and end apart: 5, of which 3 were waited for; matrix products, arithmetic and copies ran while one was open for 3% of the time, Pallas kernels for 5%

commit v1 on v0

--- a/solution.py
+++ b/solution.py
@@ -10,6 +10,7 @@
 
 SAMPLES = 64
 HIGHEST = lax.Precision.HIGHEST
+MESH = pl.DeviceIdType.MESH
 
 
 def shifted(block, axis, distance):
@@ -33,6 +34,141 @@
 
 def join3(product, rows):
     return (product[:rows] + product[rows : 2 * rows]) + product[2 * rows :]
+
+
+def greet(devices):
+    barrier = pltpu.get_barrier_semaphore()
+    for device in devices:
+        pl.semaphore_signal(barrier, inc=1, device_id=device, device_id_type=MESH)
+    pl.semaphore_wait(barrier, len(devices))
+
+
+def spread(count, position, core, partner, device_of, source_of, out_ref, sems):
+    send, recv, hand, take, own = sems
+    local = pltpu.make_async_copy(source_of(position), out_ref.at[position, core], own)
+    local.start()
+    out = []
+    for hop in range(1, count):
+        peer = (position + hop) % count
+        copy = pltpu.make_async_remote_copy(
+            src_ref=source_of(peer),
+            dst_ref=out_ref.at[position, core],
+            send_sem=send.at[hop],
+            recv_sem=recv.at[hop],
+            device_id=device_of(peer),
+            device_id_type=MESH,
+        )
+        copy.start()
+        out.append(copy)
+    handed = []
+    for hop in range(count):
+        origin = (position + count - hop) % count
+        if hop:
+            out[hop - 1].wait_recv()
+        copy = pltpu.make_async_remote_copy(
+            src_ref=source_of(position) if hop == 0 else out_ref.at[origin, core],
+            dst_ref=out_ref.at[origin, core],
+            send_sem=hand.at[hop],
+            recv_sem=take.at[hop],
+            device_id=partner,
+            device_id_type=MESH,
+        )
+        copy.start()
+        handed.append(copy)
+    for copy in handed:
+        copy.wait()
+    for copy in out:
+        copy.wait_send()
+    local.wait()
+
+
+def spread_sems(count):
+    return [pltpu.SemaphoreType.DMA((count,))] * 4 + [pltpu.SemaphoreType.DMA]
+
+
+def gather_kernel(count, flat_ref, out_ref, *sems):
+    me = lax.axis_index("tm")
+    core = me % 2
+    partner = {"tm": me + 1 - 2 * core}
+    position = me // 2
+
+    def device_of(peer):
+        return {"tm": peer * 2 + core}
+
+    greet([device_of((position + hop) % count) for hop in range(1, count)] + [partner])
+    spread(count, position, core, partner, device_of, lambda peer: flat_ref, out_ref, sems)
+
+
+def gather(flat, tm_count):
+    count = tm_count // 2
+    out = pl.pallas_call(
+        functools.partial(gather_kernel, count),
+        in_specs=[pl.BlockSpec(memory_space=pl.ANY)],
+        out_specs=pl.BlockSpec(memory_space=pl.ANY),
+        out_shape=jax.ShapeDtypeStruct((count, 2) + flat.shape, jnp.float32),
+        scratch_shapes=spread_sems(count),
+        compiler_params=pltpu.CompilerParams(collective_id=0, has_side_effects=True),
+        name="gather",
+    )(flat)
+    return out.reshape((tm_count,) + flat.shape)
+
+
+def exchange_kernel(count, tiles_ref, flags_ref, out_ref, flags_out_ref, flag_send, flag_recv, flag_own, *sems):
+    me = lax.axis_index("tm")
+    core = me % 2
+    partner = {"tm": me + 1 - 2 * core}
+    position = lax.axis_index("band")
+
+    def device_of(peer):
+        return {"band": peer}
+
+    greet([device_of((position + hop) % count) for hop in range(1, count)] + [partner])
+    own = pltpu.make_async_copy(flags_ref.at[position], flags_out_ref.at[position], flag_own)
+    own.start()
+    flags = []
+    for hop in range(1, count):
+        peer = (position + hop) % count
+        copy = pltpu.make_async_remote_copy(
+            src_ref=flags_ref.at[peer],
+            dst_ref=flags_out_ref.at[position],
+            send_sem=flag_send.at[hop],
+            recv_sem=flag_recv.at[hop],
+            device_id=device_of(peer),
+            device_id_type=MESH,
+        )
+        copy.start()
+        flags.append(copy)
+    spread(
+        count, position, core, partner, device_of, lambda peer: tiles_ref.at[peer], out_ref, sems
+    )
+    for copy in flags:
+        copy.wait()
+    own.wait()
+
+
+def exchange(tiles, flags, band_count):
+    half, rows, tile_size = tiles.shape
+    each = half // band_count
+    tiles = tiles.reshape(band_count, each, rows, tile_size)
+    flags = flags.reshape(band_count, 2 * each, tile_size)
+    out, flags_out = pl.pallas_call(
+        functools.partial(exchange_kernel, band_count),
+        in_specs=[pl.BlockSpec(memory_space=pl.ANY)] * 2,
+        out_specs=[pl.BlockSpec(memory_space=pl.ANY)] * 2,
+        out_shape=[
+            jax.ShapeDtypeStruct((band_count, 2, each, rows, tile_size), jnp.float32),
+            jax.ShapeDtypeStruct(flags.shape, jnp.float32),
+        ],
+        scratch_shapes=[
+            pltpu.SemaphoreType.DMA((band_count,)),
+            pltpu.SemaphoreType.DMA((band_count,)),
+            pltpu.SemaphoreType.DMA,
+        ]
+        + spread_sems(band_count),
+        compiler_params=pltpu.CompilerParams(collective_id=1, has_side_effects=True),
+        name="exchange",
+    )(tiles, flags)
+    return out.reshape(2 * half, rows, tile_size), flags_out.reshape(2 * half, tile_size)
 
 
 def pick_kernel(slots_ref, shards_ref, rise_ref, fall_ref):
@@ -96,13 +232,13 @@
         out_ref[0] = jnp.where(taken > 0.0, join3(product, rows), tile_ref[0])
 
 
-def place(whole, slots_column, climbers, sinkers, route, tile_size):
+def place(whole, slots_column, climbers, sinkers, route, tile_size, crossing_tiles):
     _, rows, width = whole.shape
     ranks = slots_column.shape[0]
     tile_count = route.shape[0]
     per_shard = width // tile_size
     return pl.pallas_call(
-        functools.partial(place_kernel, tile_count // 2),
+        functools.partial(place_kernel, crossing_tiles),
         grid_spec=pltpu.PrefetchScalarGridSpec(
             num_scalar_prefetch=1,
             grid=(tile_count,),
@@ -217,18 +353,21 @@
     row_start = lax.axis_index("tm") * share
 
     flat = chebyshev.transpose(1, 0, 2).reshape(3 * orders, local)
-    whole = lax.all_gather(flat, "tm", axis=0, tiled=False)
+    whole = gather(flat, tm_count)
 
     slot_ids = jnp.arange(tile_size, dtype=jnp.int32)[None, :] + tile_size * route[0][:, None]
     alive_out = (slot_ids < counts[0]).astype(jnp.float32)
-    alive = lax.all_to_all(alive_out, "band", split_axis=0, concat_axis=0, tiled=True)
 
     slots_column = crossing[0].reshape(-1, 1)
     rising, falling = pick(whole, slots_column, (tm_count + 1) // 2)
     climbers = shifted(rising, "band", 1)
     sinkers = shifted(falling, "band", -1)
-    outgoing = place(whole, slots_column, climbers, sinkers, route[0], tile_size)
-    tiles = lax.all_to_all(outgoing, "band", split_axis=0, concat_axis=0, tiled=True)
+    band_count = lax.axis_size("band")
+    core = lax.axis_index("tm") % 2
+    halves = route[0].reshape(band_count, 2, tile_count // band_count // 2)
+    mine = lax.dynamic_index_in_dim(halves, core, 1, keepdims=False).reshape(-1)
+    outgoing = place(whole, slots_column, climbers, sinkers, mine, tile_size, tile_count // 2)
+    tiles, alive = exchange(outgoing, alive_out, band_count)
     return pair_blocks(tiles, alive, pairs[0, 0], pairs[0, 1], row_start, share)
 
 

time: 173 us -> 144 us (0.83)
  the two profiles are of different devices: /device:TPU:4 before, /device:TPU:25 now
where the time goes in v1:
time: 144 us
  Pallas kernels  119 us (83%)
  local copies, waits for them, and re-layouts  12.3 us (9%)
  waiting for transfers between devices  5.5 us (4%)
  starting transfers between devices  4.41 us (3%)
  other arithmetic  2.24 us (2%)
    pallas_call x1, Pallas kernels, pair_blocks(): pl.pallas_call(functools.partial(pair_kernel, share), grid_spec=pltpu.Pre...  46.3 us
    pallas_call x1, Pallas kernels, gather(): pl.pallas_call(functools.partial(gather_kernel, count), in_specs=[pl.Bloc...  40.3 us
    pallas_call x1, Pallas kernels, exchange(): pl.pallas_call(functools.partial(exchange_kernel, band_count), in_specs=[...  23.3 us
    unnamed x23, local copies, waits for them, and re-layouts  10.4 us
    ppermute x2, waiting for transfers between devices, shifted(): return lax.ppermute(block, axis, route)  5.5 us
    pallas_call x1, Pallas kernels, place(): pl.pallas_call(functools.partial(place_kernel, crossing_tiles), grid_spec...  5.49 us
    ppermute x2, starting transfers between devices, shifted(): return lax.ppermute(block, axis, route)  4.41 us
    pallas_call x1, Pallas kernels, pick(): pl.pallas_call(pick_kernel, grid=(1,), in_specs=[pl.BlockSpec((ranks, 1),...  3.4 us
  transfers between devices with their start and end apart: 2, of which 1 were waited for; matrix products, arithmetic and copies ran while one was open for 2% of the time, Pallas kernels for 0%

profile of v1, /device:TPU:25, one launch (start us, length us, event | category | flops | bytes accessed | tf_op | source)
XLA Modules:
  0.0 144.0 jit_solution(3215477070291861406)
XLA Ops:
  0.0 0.0 copy-start.8
  0.0 0.0 copy-start.9
  0.0 40.3 %gather.1 = f32[4,2,96,1024]{3,2,1,0:T(8,128)} custom-call(f32[96,1024]{1,0:T(8,128)} %bitcast.24), custom_call_target="tpu_custom_call" | custom-call | tf_op jit(solution)/shard_map/gather/pallas_call | solution.py:104
  40.3 0.0 copy-done.8
  40.3 1.0 copy.11
  41.4 0.0 copy-start
  41.4 1.9 %copy-done = f32[4,2,96,1024]{3,2,1,0:T(8,128)S(1)} copy-done((f32[4,2,96,1024]{3,2,1,0:T(8,128)S(1)}, f32[4,2,96,1024]{3,2,1,0:T(8,128)}, u32[]{:S(2)}) %copy-start) | copy-done | bytes 3145752
  43.3 0.0 copy-start.4
  43.3 1.0 copy-done.4
  44.3 0.0 copy-start.1
  44.3 3.4 %pick.1 = (f32[96,512]{1,0:T(8,128)}, f32[96,512]{1,0:T(8,128)}) custom-call(s32[1024,1]{1,0:T(8,128)S(1)} %bitcast.22, f32[8,96,1024]{2,1,0:T(8,128)S(1)} %bitcast.17), custom_call_target="tpu_custom_call" | custom-call | tf_op jit(solution)/shard_map/pick/pallas_call | solution.py:196
  47.7 3.1 %collective-permute-start = (f32[96,512]{1,0:T(8,128)}, f32[96,512]{1,0:T(8,128)S(1)}, u32[]{:S(2)}, u32[]{:S(2)}) collective-permute-start(f32[96,512]{1,0:T(8,128)} %get-tuple-element.9), channel_id=1, source_target_pairs={{0,8},{8,16},{16,24},{1,9},{9,17},{17,25},{2,10},{10,18},{18,26},{... | collective-permute-start | bytes 589832 | tf_op jit(solution)/shard_map/ppermute | solution.py:19
  50.8 1.3 collective-permute-start.1
  52.1 0.6 broadcast.27
  52.7 0.0 copy-done.9
  52.7 0.6 multiply_reduce_fusion
  53.4 0.1 reshape_squeeze.6
  53.5 0.1 reshape.40.route_ref
  53.6 0.1 mul.19
  54.3 0.7 fusion.flags_ref
  55.0 0.1 pad_add_fusion.place_ref
  55.1 0.8 slice_bitcast_fusion
  55.8 0.0 collective-permute-done.rise_ref
  55.8 5.5 %collective-permute-done.1.fall_ref = f32[96,512]{1,0:T(8,128)S(1)} collective-permute-done((f32[96,512]{1,0:T(8,128)}, f32[96,512]{1,0:T(8,128)S(1)}, u32[]{:S(2)}, u32[]{:S(2)}) %collective-permute-start.1) | collective-permute-done | bytes 196640 | tf_op jit(solution)/shard_map/ppermute | solution.py:19
  61.3 0.0 copy-done.1
  61.3 0.0 copy-start.5
  61.3 1.0 copy-done.5
  62.4 5.5 %place.1 = f32[16,96,256]{2,1,0:T(8,128)S(1)} custom-call(s32[16]{0:T(128)S(1)} %reshape.40.route_ref, s32[1024,1]{1,0:T(8,128)S(1)} %bitcast.23, f32[8,96,1024]{2,1,0:T(8,128)S(1)} %bitcast.18, f32[96,512]{1,0:T(8,128)S(1)} %collective-permute-done.rise_ref, f32[96,512]{1,0:T(8,128)S(1)} %collective-permute-done.1.fall_ref), custom_call_target="tpu_custom_call" | custom-call | tf_op jit(solution)/shard_map/place/pallas_call | solution.py:240
  67.9 0.0 copy-start.3
  67.9 1.1 copy-done.3
  69.0 23.3 %exchange.1 = (f32[4,2,4,96,256]{4,3,2,1,0:T(8,128)}, f32[4,8,256]{2,1,0:T(8,128)}) custom-call(f32[4,4,96,256]{3,2,1,0:T(8,128)} %bitcast.21, f32[4,8,256]{2,1,0:T(8,128)} %fusion.flags_ref), custom_call_target="tpu_custom_call" | custom-call | tf_op jit(solution)/shard_map/exchange/pallas_call | solution.py:154
  92.3 0.8 reshape_reshape.3.alive_window_ref.alive_tile_ref
  93.1 0.8 reduce_max.9
  94.0 0.1 reshape.45.live
  94.1 0.0 copy-start.2
  94.1 1.9 %copy-done.2 = f32[4,2,4,96,256]{4,3,2,1,0:T(8,128)S(1)} copy-done((f32[4,2,4,96,256]{4,3,2,1,0:T(8,128)S(1)}, f32[4,2,4,96,256]{4,3,2,1,0:T(8,128)}, u32[]{:S(2)}) %copy-start.2) | copy-done | bytes 3145752
  96.0 0.0 copy-start.6
  96.0 0.9 copy-done.6
  96.9 0.0 copy-start.7
  96.9 0.9 copy-done.7
  97.8 46.3 %pair_blocks.1 = f32[32,32,256]{2,1,0:T(8,128)} custom-call(s32[32]{0:T(128)S(1)} %get-tuple-element.16.first_ids, s32[32]{0:T(128)S(1)} %get-tuple-element.15.second_ids, s32[32]{0:T(128)S(1)} %reshape.45.live, s32[2]{0:T(128)S(1)} %pad_add_fusion.place_ref, f32[32,96,256]{2,1,0:T(8,128)S(1)} %bitcast.19, f32[32,96,256]{2,1,0:T(8,128)S(1)} %bitcast.20, ...), custom_call_target="tpu_custom_call" | custom-call | tf_op jit(solution)/shard_map/pair_blocks/pallas_call | solution.py:320
  (3 shorter events, 0.0 us)
Async XLA Ops:
  0.0 40.3 %copy-start.8 = (s32[1,2,512]{2,1,0:T(2,128)S(1)}, s32[1,2,512]{2,1,0:T(2,128)}, u32[]{:S(2)}) copy-start(s32[1,2,512]{2,1,0:T(2,128)} %param.8) | copy-start | bytes 12292
  0.0 52.7 %copy-start.9 = (s32[1,32]{1,0:T(1,128)S(1)}, s32[1,32]{1,0:T(1,128)}, u32[]{:S(2)}) copy-start(s32[1,32]{1,0:T(1,128)} %param.10) | copy-start | bytes 388
  41.4 1.9 %copy-start = (f32[4,2,96,1024]{3,2,1,0:T(8,128)S(1)}, f32[4,2,96,1024]{3,2,1,0:T(8,128)}, u32[]{:S(2)}) copy-start(f32[4,2,96,1024]{3,2,1,0:T(8,128)} %gather.1) | copy-start | bytes 9437188
  43.3 1.0 copy-start.4
  44.3 17.0 %copy-start.1 = (f32[4,2,96,1024]{3,2,1,0:T(8,128)S(1)}, f32[4,2,96,1024]{3,2,1,0:T(8,128)}, u32[]{:S(2)}) copy-start(f32[4,2,96,1024]{3,2,1,0:T(8,128)} %gather.1) | copy-start | bytes 9437188
  47.7 8.1 %collective-permute-start = (f32[96,512]{1,0:T(8,128)}, f32[96,512]{1,0:T(8,128)S(1)}, u32[]{:S(2)}, u32[]{:S(2)}) collective-permute-start(f32[96,512]{1,0:T(8,128)} %get-tuple-element.9), channel_id=1, source_target_pairs={{0,8},{8,16},{16,24},{1,9},{9,17},{17,25},{2,10},{10,18},{18,26},{... | collective-permute-start | bytes 589832 | tf_op jit(solution)/shard_map/ppermute | solution.py:19
  50.8 10.5 %collective-permute-start.1 = (f32[96,512]{1,0:T(8,128)}, f32[96,512]{1,0:T(8,128)S(1)}, u32[]{:S(2)}, u32[]{:S(2)}) collective-permute-start(f32[96,512]{1,0:T(8,128)} %get-tuple-element.10), channel_id=1, source_target_pairs={{8,0},{16,8},{24,16},{9,1},{17,9},{25,17},{10,2},{18,10},{26,18},{... | collective-permute-start | bytes 589832 | tf_op jit(solution)/shard_map/ppermute | solution.py:19
  61.3 1.0 copy-start.5
  67.9 1.1 copy-start.3
  94.1 1.9 %copy-start.2 = (f32[4,2,4,96,256]{4,3,2,1,0:T(8,128)S(1)}, f32[4,2,4,96,256]{4,3,2,1,0:T(8,128)}, u32[]{:S(2)}) copy-start(f32[4,2,4,96,256]{4,3,2,1,0:T(8,128)} %get-tuple-element.12) | copy-start | bytes 9437188
  96.0 0.9 copy-start.6
  96.9 0.9 copy-start.7
